TPU v7x, 32 devices: a whole 2x2x4 slice. The times are simulated.
32 devices in a mesh: frow: 4 (over y, x), fcol: 8 (over z, core).
Axes of the slice: x: 2, y: 2, z: 4, core: 2. Of those that a mesh axis runs over, the one named last changes fastest.
Arguments:
- vis: float32 [2, 8192], P(None, ('frow', 'fcol')), may hold values from -6 to 6
- station_pairs: int32 [2, 8192], P(None, ('frow', 'fcol')), may hold values from 0 to 511
- visibility_time_slot: int32 [8192], P(('frow', 'fcol')), may hold values from 0 to 15
- station_u_cells: int32 [512], replicated, may hold values from -1024 to 1023
- station_v_cells: int32 [512], replicated, may hold values from -1024 to 1023
- facet_station_gains: float32 [4, 8, 2, 8192], P('frow', 'fcol'), may hold values from -6 to 6
- holder_device_order: int32 [32], replicated, may hold values from 0 to 31, each once
Outputs:
- image: float32 [4096, 4096], P('frow', 'fcol')
Inputs may be any that keep to these rules, and one draw needn't show every extreme that they name: `holder_device_order`: a permutation; its first 4 entries name distinct devices.
All inputs are finite; a program needn't handle non-finite values.
Results may differ from a plain program's by a relative error of at most 0.0037.
Values sent between devices are 32-bit elements; how exact they have to be, the bound alone decides.
No kernel may reach another device: no remote copies, remote signals or barrier semaphores. Data moves between devices by JAX's collectives and lax.ppermute only.
A program may use at most 64 MiB of HBM per device.

v0:
```python
import functools
import math

import jax
import jax.numpy as jnp
from jax import lax
from jax.experimental import pallas as pl
from jax.experimental.pallas import tpu as pltpu
from jax.sharding import PartitionSpec as P

R = 1024
C = 512
M = 64
NT = 16
NBLK = 4
LANES = 128
SUB = 8
OWN, LEFT, RIGHT, UP, DOWN, UL, UR, DL, DR = range(9)
F32 = jnp.float32
BF16 = jnp.bfloat16


def wrap(m, modulus):
    if modulus & (modulus - 1) == 0:
        return m & (modulus - 1)
    return jnp.remainder(m, modulus)


def turn(m, modulus):
    m = wrap(m, modulus)
    quarter = modulus // 4
    q = (m + modulus // 8) // quarter if quarter & (quarter - 1) else (
        (m + modulus // 8) >> (quarter.bit_length() - 1))
    x = (m - q * quarter).astype(F32) * (2.0 * math.pi / modulus)
    x2 = x * x
    s = x + x * x2 * (-1 / 6 + x2 * (1 / 120 + x2 * (-1 / 5040 + x2 * (1 / 362880))))
    c = 1.0 + x2 * (-0.5 + x2 * (1 / 24 + x2 * (-1 / 720 + x2 * (1 / 40320))))
    odd = (q & 1) == 1
    cos = jnp.where(odd, s, c)
    sin = jnp.where(odd, c, s)
    cos = jnp.where(((q + 1) & 2) != 0, -cos, cos)
    sin = jnp.where((q & 2) != 0, -sin, sin)
    return cos, sin


def times(a, b):
    return a[0] * b[0] - a[1] * b[1], a[0] * b[1] + a[1] * b[0]


def pack_kernel(order_ref, vis_ref, pair_ref, slot_ref, u_ref, v_ref, out_ref, label_ref):
    block = vis_ref.shape[1]
    lines = [vis_ref[0:1, :], vis_ref[1:2, :], pair_ref[0:1, :].astype(F32),
             pair_ref[1:2, :].astype(F32), slot_ref[...].astype(F32)]
    for copy in range(out_ref.shape[0]):
        for q, line in enumerate(lines):
            out_ref[copy, :, q * block:(q + 1) * block] = line
    n_lines = u_ref.shape[0]
    at = lax.broadcasted_iota(jnp.int32, (SUB, LANES), 1)
    order = jnp.zeros((SUB, LANES), jnp.int32)
    for b in range(NBLK):
        order = jnp.where(at == b, order_ref[b], order)
    label_ref[:SUB] = order.astype(F32)
    label_ref[SUB:SUB + n_lines] = u_ref[...].astype(F32)
    label_ref[SUB + n_lines:SUB + 2 * n_lines] = v_ref[...].astype(F32)


def pick(row, lane):
    return jnp.take_along_axis(
        jnp.broadcast_to(row, lane.shape), lane, axis=1, mode="promise_in_bounds")


def taper_rows(group, half, wide=LANES):
    index = (lax.broadcasted_iota(jnp.int32, (SUB, wide), 0) + SUB * group).astype(F32)
    return ((half + M - 0.5 - index) * (1.0 / (2 * M)),
            (index - (half - M - 0.5)) * (1.0 / (2 * M)))


def phase_tables(n_frow, n_fcol, first, n_lines, block_ref, cell_ref,
                 s_ref, ac_ref, as_ref, ec_ref, es_ref, fc_ref, fs_ref, cc_ref, cs_ref,
                 q_ref, uv_ref, dr_ref):
    frow_at = lax.axis_index("frow")
    fcol_at = lax.axis_index("fcol")
    half_r, half_c = R // 2, C // 2
    mod_r, mod_c = 2 * R * n_frow, 2 * C * n_fcol
    k_tiles = s_ref.shape[1]
    per_block = k_tiles // NBLK
    block = per_block * LANES
    shape = (SUB, LANES)

    order = cell_ref[first:first + 1, :]
    place = lax.broadcasted_iota(jnp.int32, (1, LANES), 1)
    owners = [jnp.sum(jnp.where(place == b, order, 0.0)).astype(jnp.int32) for b in range(NBLK)]
    for b, owner in enumerate(owners):
        for q in range(5):
            for j in range(per_block):
                q_ref[q, b * per_block + j:b * per_block + j + 1, :] = block_ref[
                    owner, :, q * block + j * LANES:q * block + (j + 1) * LANES]
    a1 = q_ref[2].astype(jnp.int32)
    a2 = q_ref[3].astype(jnp.int32)
    slot = q_ref[4].astype(jnp.int32)

    at = first + SUB

    def cells(table):
        got = [jnp.zeros(shape, F32)] * 2
        for h in range(table.shape[0]):
            row = table[h:h + 1, :]
            got = [jnp.where((a >> 7) == h, pick(row, a & 127), g)
                   for a, g in zip((a1, a2), got)]
        return (got[0] - got[1]).astype(jnp.int32)

    u = cells(cell_ref[at:at + n_lines, :])
    v = cells(cell_ref[at + n_lines:at + 2 * n_lines, :])
    uv_ref[0] = u
    uv_ref[1] = v
    centre = times(turn(u * (frow_at * (2 * R) + (R - 1)), mod_r),
                   turn(v * (fcol_at * (2 * C) + (C - 1)), mod_c))
    scale = 0.5 / math.sqrt(NBLK * per_block * LANES)
    value = times((q_ref[0] * scale, q_ref[1] * scale), centre)
    s_ref[0] = value[0]
    s_ref[1] = value[1]
    for n, a in enumerate((a1, a2)):
        s_ref[2 + n] = ((a >> 3) + (a & 6) * 32).astype(F32)
        s_ref[4 + n] = ((a & 1) * NT + slot).astype(F32)

    iota = lax.broadcasted_iota(jnp.int32, shape, 0)

    def tables(s):
        lane = slice(s * LANES, (s + 1) * LANES)

        def phases(which, modulus, half):
            freq = jnp.broadcast_to(uv_ref[which, s:s + 1, :], shape)
            fine = turn(freq * (2 * iota + 1), modulus)
            middle = turn(freq * (16 * iota), modulus)
            coarse = turn(freq * (128 * iota), modulus)
            for a in range(half // 64):
                top = tuple(jnp.broadcast_to(x[a:a + 1], shape) for x in coarse)
                both = times(middle, top)
                for comp in range(2):
                    dr_ref[s, which, comp, 8 * a:8 * a + 8, :] = both[comp]
            for g in range(half // SUB):
                step = tuple(jnp.broadcast_to(dr_ref[s, which, comp, g:g + 1, :], shape)
                             for comp in range(2))
                yield times(fine, step)

        pairs = {}

        def put(ref, first, group, x):
            key = (id(ref), first)
            if group % 2 == 0:
                pairs[key] = x
            else:
                start = first + SUB * (group - 1)
                ref[start:start + 16, lane] = jnp.concatenate([pairs.pop(key), x], 0).astype(BF16)

        edge = (half_r - M) // SUB
        for g, (cos, sin) in enumerate(phases(0, mod_r, half_r)):
            if g >= edge:
                mine, other = taper_rows(g, half_r)
                at = slice((g - edge) * SUB, (g - edge + 1) * SUB)
                ec_ref[at, lane] = cos * other
                es_ref[at, lane] = sin * other
                cos, sin = cos * mine, sin * mine
            put(ac_ref, 0, g, cos)
            put(as_ref, 0, g, sin)
        for g, (cos, sin) in enumerate(phases(1, mod_c, half_c)):
            put(cc_ref, 0, g, cos)
            put(cs_ref, 0, g, sin)
            at = slice(g * SUB, (g + 1) * SUB)
            fc_ref[at, lane] = cos
            fs_ref[at, lane] = sin

    return tables


def gain_kernel(depth, mid_ref, a_ref, b_ref, gain_ref):
    half = depth // 2
    places = 2 * NT
    low_lane = lax.broadcasted_iota(jnp.int32, (places, LANES), 1) < LANES // 2
    for f in range(9):
        ref, row = (mid_ref, a_ref, b_ref)[f // 3], f % 3 * depth
        both = jnp.concatenate([ref[pl.ds(row, half, stride=2), :],
                                ref[pl.ds(row + 1, half, stride=2), :]], 0).T
        quarter = [both[i * places:(i + 1) * places] for i in range(4)]
        turned = [pltpu.roll(x, LANES // 2, 1) for x in quarter]
        for t in range(2):
            re = jnp.where(low_lane, quarter[2 * t], turned[2 * t + 1])
            im = jnp.where(low_lane, turned[2 * t], quarter[2 * t + 1])
            for comp, x in enumerate((re, im)):
                high = x.astype(BF16)
                at = (2 * (f - 1 if f else SUB) + comp) * places
                gain_ref[at:at + places, t * LANES:(t + 1) * LANES] = high
                if f == 0:
                    at += 2 * places
                    gain_ref[at:at + places, t * LANES:(t + 1) * LANES] = (
                        x - high.astype(F32)).astype(BF16)


def image_kernel(n_frow, n_fcol, first, n_lines, depth, block_ref, cell_ref, gain_ref, image_ref,
                 s_ref, ac_ref, as_ref, ec_ref, es_ref, fc_ref, fs_ref, cc_ref, cs_ref,
                 q_ref, uv_ref, dr_ref, out_ref, tc_ref, ts_ref, uc_ref, us_ref, w_ref,
                 m1_ref, m2_ref, g1_ref, g2_ref, sems):
    tables = phase_tables(n_frow, n_fcol, first, n_lines, block_ref, cell_ref, s_ref, ac_ref,
                          as_ref, ec_ref, es_ref, fc_ref, fs_ref, cc_ref, cs_ref,
                          q_ref, uv_ref, dr_ref)
    frow_at = lax.axis_index("frow")
    r_odd = lax.rem(frow_at, 2) == 1
    fcol_at = lax.axis_index("fcol")
    c_odd = lax.rem(fcol_at, 2) == 1
    k_tiles = s_ref.shape[1]
    half_c = C // 2
    places = 2 * NT

    r_first, r_second = jnp.where(r_odd, 1, 2), jnp.where(r_odd, 2, 1)
    c_first, c_second = jnp.where(c_odd, 1, 2), jnp.where(c_odd, 2, 1)
    rows = {UP: r_first - 1, DOWN: r_second - 1, LEFT: 3 * c_first - 1, RIGHT: 3 * c_second - 1,
            UL: 3 * c_first + r_first - 1, UR: 3 * c_second + r_first - 1,
            DL: 3 * c_first + r_second - 1, DR: 3 * c_second + r_second - 1}

    step = 2 if k_tiles % 2 == 0 else 1
    wide = step * LANES
    shape = (SUB, wide)
    line_at = lax.broadcasted_iota(jnp.int32, (2 * depth, wide), 0).astype(F32)
    place_at = line_at[:places]
    row_at = lax.broadcasted_iota(jnp.int32, shape, 0)
    zero = jnp.zeros((M, wide), BF16)
    r_edge = jnp.logical_or(frow_at == 0, frow_at == n_frow - 1)
    c_edge = jnp.logical_or(fcol_at == 0, fcol_at == n_fcol - 1)
    keep = (jnp.where(lax.rem(row_at, 3) == 1, jnp.where(r_edge, 0.0, 1.0), 1.0)
            * jnp.where(row_at >= 5, jnp.where(c_edge, 0.0, 1.0), 1.0))

    def fold(parts):
        parts = [parts[i] for i in (0, 4, 2, 6, 1, 5, 3, 7)]
        for distance in (1, 2, 4):
            low = (row_at & distance) == 0
            count = len(parts) // 2
            parts = [jnp.where(low, x, y) + pltpu.roll(jnp.where(low, y, x), distance, 0)
                     for x, y in zip(parts[:count], parts[count:])]
        return parts[0]

    def gain_product(first, second):
        (g1r, g1i), (g2r, g2i) = first, second
        return g1r * g2r + g1i * g2i, g1i * g2r - g1r * g2i

    def weight(f, lane):
        return tuple(jnp.broadcast_to(w_ref[comp, pl.ds(rows[f], 1), lane], shape)
                     for comp in range(2))

    for p in range(k_tiles // step):
        lane = slice(p * wide, (p + 1) * wide)

        def line(q):
            return jnp.concatenate([s_ref[q, p * step + i:p * step + i + 1, :]
                                    for i in range(step)], 1)

        for i in range(step):
            tables(p * step + i)
        owns, nears = [], []
        for n in range(2):
            hot = jnp.where(line_at == line(2 + n), 1.0, 0.0).astype(BF16)
            mask = jnp.where(place_at == line(4 + n), 1.0, 0.0)
            z = jnp.dot(gain_ref[...], hot, preferred_element_type=F32)

            def part(f, comp):
                at = (2 * f + comp) * places
                x = z[at:at + places]
                if f == SUB:
                    x = x + z[at + 2 * places:at + 3 * places]
                x = x * mask
                return sum((x[i * SUB:(i + 1) * SUB] for i in range(1, places // SUB)), x[:SUB])

            owns.append([jnp.sum(part(SUB, comp), axis=0, keepdims=True) for comp in range(2)])
            nears.append([fold([part(f, comp) for f in range(SUB)]) for comp in range(2)])
        value = (line(0), line(1))
        own_w = times(value, gain_product(*owns))
        near_w = times(tuple(x * keep for x in value), gain_product(*nears))
        for comp in range(2):
            w_ref[comp, :, lane] = near_w[comp]

        pairs = {}

        def put(ref, first, group, x):
            key = (id(ref), first)
            if group % 2 == 0:
                pairs[key] = x
            else:
                start = first + SUB * (group - 1)
                ref[start:start + 16, lane] = jnp.concatenate([pairs.pop(key), x], 0).astype(BF16)

        edge = (half_c - M) // SUB
        wr, wi = [jnp.broadcast_to(x, shape) for x in own_w]
        (lr, li), (rr, ri) = weight(LEFT, lane), weight(RIGHT, lane)
        for g in range(half_c // SUB):
            at = slice(g * SUB, (g + 1) * SUB)
            cos, sin = fc_ref[at, lane], fs_ref[at, lane]
            own = (cos, sin)
            if g >= edge:
                mine, other = taper_rows(g, half_c, wide)
                own = (cos * mine, sin * mine)
                cos, sin = cos * other, sin * other
                base = 2 * half_c + M
                put(tc_ref, base, g - edge, lr * cos + li * sin)
                put(ts_ref, base, g - edge, lr * sin - li * cos)
                put(tc_ref, base + 2 * M, g - edge, rr * cos - ri * sin)
                put(ts_ref, base + 2 * M, g - edge, -(rr * sin + ri * cos))
            base = g * SUB // LANES * LANES
            put(tc_ref, base, g, wr * own[0])
            put(tc_ref, base + LANES, g, -wi * own[1])
            put(ts_ref, base, g, -wi * own[0])
            put(ts_ref, base + LANES, g, -wr * own[1])
        for ref in (tc_ref, ts_ref):
            ref[2 * half_c:2 * half_c + M, lane] = zero
            ref[2 * half_c + 2 * M:2 * half_c + 3 * M, lane] = zero

    def dot(a, b):
        return lax.dot_general(a, b, (((1,), (1,)), ((), ())), preferred_element_type=F32)

    half_r = R // 2
    n_lane = half_c // LANES

    def own_products(t):
        cols = slice(2 * t * LANES, 2 * (t + 1) * LANES if t < n_lane - 1 else tc_ref.shape[0])
        m1_ref[:, cols] = dot(ac_ref[...], tc_ref[cols, :])
        m2_ref[:, cols] = dot(as_ref[...], ts_ref[cols, :])

    own_products(n_lane - 1)
    signs = (-1, 1, -1, -1, 1, 1)
    for p in range(k_tiles // step):
        lane = slice(p * wide, (p + 1) * wide)
        for n, (f, sd) in enumerate(zip((UP, DOWN, UL, UR, DL, DR), signs)):
            wr, wi = weight(f, lane)
            for g in range(0, M // SUB, 2):
                tops, lows = [], []
                for i in range(2):
                    at = slice((g + i) * SUB, (g + i + 1) * SUB)
                    cos, sin = ec_ref[at, lane], es_ref[at, lane]
                    tops.append(wr * cos - (sd * wi) * sin)
                    lows.append(-(sd * wr) * sin - wi * cos)
                at = slice(n * M + g * SUB, n * M + (g + 2) * SUB)
                uc_ref[at, lane] = jnp.concatenate(tops, 0).astype(BF16)
                us_ref[at, lane] = jnp.concatenate(lows, 0).astype(BF16)
    g1_ref[...] = dot(uc_ref[...], cc_ref[...])
    g2_ref[...] = dot(us_ref[...], cs_ref[...])

    shape = (SUB, LANES)
    iota = lax.broadcasted_iota(jnp.int32, shape, 0)
    lane_at = lax.broadcasted_iota(jnp.int32, shape, 1)
    back_lane = (LANES - 1) - lane_at
    back_row = (SUB - 1) - iota
    edge_c = half_c - M
    edge_r = half_r - M
    col_own, col_other = [], []
    for t in range(n_lane):
        index = (lane_at + t * LANES).astype(F32)
        col_own.append(jnp.minimum((half_c + M - 0.5 - index) * (1.0 / (2 * M)), 1.0))
        col_other.append(jnp.maximum((index - (half_c - M - 0.5)) * (1.0 / (2 * M)), 0.0))

    def flip(x, index, axis):
        return jnp.take_along_axis(x, index, axis=axis, mode="promise_in_bounds")

    def finish(g, t, edged):
        rows = slice(g * SUB, (g + 1) * SUB)
        def part(ref, which):
            return ref[rows, (2 * t + which) * LANES:(2 * t + which + 1) * LANES]
        p, s_, r, q = part(m1_ref, 0), part(m1_ref, 1), part(m2_ref, 0), part(m2_ref, 1)
        even, odd = p + q, p - q
        plus, minus = r + s_, r - s_
        quad = {(1, 1): even + plus, (-1, -1): even - plus,
                (1, -1): odd + minus, (-1, 1): odd - minus}
        if (t + 1) * LANES > edge_c:
            base = 2 * half_c
            off = t * LANES - (half_c - LANES)
            for se, start in ((-1, base), (1, base + LANES)):
                lc = m1_ref[rows, start + off:start + off + LANES]
                ls = m2_ref[rows, start + off:start + off + LANES]
                quad[1, se] += lc + ls
                quad[-1, se] += lc - ls
        if edged:
            def edge(n):
                at = slice(n * M + g * SUB - edge_r, n * M + (g + 1) * SUB - edge_r)
                x = g1_ref[at, t * LANES:(t + 1) * LANES]
                y = g2_ref[at, t * LANES:(t + 1) * LANES]
                return {1: x + y, -1: x - y}
            for n, sd in ((0, -1), (1, 1)):
                e = edge(n)
                for se in (-1, 1):
                    quad[sd, se] += e[se] * col_own[t]
            if (t + 1) * LANES > edge_c:
                for n, (sd, se) in ((2, (-1, -1)), (3, (-1, 1)), (4, (1, -1)), (5, (1, 1))):
                    quad[sd, se] += edge(n)[se] * col_other[t]
        for (sd, se), x in quad.items():
            if sd < 0:
                x = flip(x, back_row, 0)
                at = slice(half_r - SUB - g * SUB, half_r - g * SUB)
            else:
                at = slice(half_r + g * SUB, half_r + (g + 1) * SUB)
            if se < 0:
                x = flip(x, back_lane, 1)
                start = half_c - (t + 1) * LANES
            else:
                start = half_c + t * LANES
            out_ref[at, start:start + LANES] = x

    n_groups = half_r // M

    def sends(j, t):
        copies = []
        for row in (half_r + 2 * M * j, half_r - 2 * M * (j + 1)):
            for col in (half_c + t * LANES, half_c - (t + 1) * LANES):
                at = (slice(row, row + 2 * M), slice(col, col + LANES))
                copies.append(pltpu.make_async_copy(
                    out_ref.at[at], image_ref.at[at], sems.at[(j * n_lane + t) * 4 + len(copies)]))
        return copies

    for t in range(n_lane - 2, -1, -1):
        own_products(t)
    for t in range(n_lane - 1, -1, -1):
        for j in range(n_groups):
            for g in range(j * M // SUB, (j + 1) * M // SUB):
                finish(g, t, j == n_groups - 1)
            if j % 2:
                for copy in sends(j // 2, t):
                    copy.start()
    for t in range(n_lane):
        for j in range(n_groups // 2):
            for copy in sends(j, t):
                copy.wait()


def swaps(size):
    both = []
    for first in (0, 1):
        pairs = [(i, i + 1) for i in range(first, size - 1, 2)]
        both.append(pairs + [(j, i) for i, j in pairs])
    return both


def all_paired(pairs, count, other):
    swap = dict(pairs)
    for i in range(count):
        if i not in swap and other(i) not in swap:
            swap[i], swap[other(i)] = other(i), i
    return list(swap.items())


def shards(vis, station_pairs, visibility_time_slot, station_u_cells, station_v_cells,
           facet_station_gains, holder_device_order):
    n_frow = lax.axis_size("frow")
    n_fcol = lax.axis_size("fcol")
    block = vis.shape[1]
    k_tiles = NBLK * block // LANES
    k = k_tiles * LANES
    half_r, half_c = R // 2, C // 2
    wide = 2 * half_c + 4 * M
    vmem = pl.BlockSpec(memory_space=pltpu.VMEM)
    smem = pl.BlockSpec(memory_space=pltpu.SMEM)

    def lines(x):
        return x.reshape(-1, LANES)

    def shaped(*dims, dtype=F32):
        return jax.ShapeDtypeStruct(dims, dtype)

    def params(mib):
        return pltpu.CompilerParams(vmem_limit_bytes=mib * 1024 * 1024)

    n_lines = station_u_cells.size // LANES
    packed, labels = pl.pallas_call(
        pack_kernel,
        out_shape=[shaped(n_frow * n_fcol, 1, 5 * block), shaped(SUB + 2 * n_lines, LANES)],
        in_specs=[smem] + [vmem] * 5,
        name="pack",
    )(holder_device_order, vis, station_pairs, visibility_time_slot.reshape(1, block),
      lines(station_u_cells), lines(station_v_cells))
    facet_station_gains, packed = lax.optimization_barrier((facet_station_gains, packed))
    gains = facet_station_gains[0, 0]
    depth = gains.size // LANES
    own = gains.reshape(2, -1, LANES).transpose(1, 0, 2).reshape(depth, LANES)
    row_a, row_b = [lax.ppermute(own, "frow", all_paired(pairs, n_frow, lambda r: n_frow - 1 - r))
                    for pairs in swaps(n_frow)]
    blocks = lax.all_to_all(packed, ("frow", "fcol"), 0, 0)
    mid = jnp.concatenate([own, row_a, row_b, labels], 0)
    count = n_frow * n_fcol

    def next_row(i):
        j = i ^ n_fcol if n_fcol & (n_fcol - 1) == 0 else i
        return j if j < count else i

    col_a, col_b = [
        lax.ppermute(mid, ("frow", "fcol"), all_paired(
            [(r * n_fcol + i, r * n_fcol + j) for r in range(n_frow) for i, j in pairs],
            count, next_row))
        for pairs in swaps(n_fcol)]
    looked = pl.pallas_call(
        functools.partial(gain_kernel, depth),
        out_shape=shaped(40 * NT, 2 * depth, dtype=BF16),
        in_specs=[vmem] * 3,
        out_specs=vmem,
        compiler_params=params(8),
        name="gains",
    )(mid, col_a, col_b)
    return pl.pallas_call(
        functools.partial(image_kernel, n_frow, n_fcol, 3 * depth, n_lines, depth),
        out_shape=shaped(R, C),
        in_specs=[vmem] * 3,
        out_specs=pl.BlockSpec(memory_space=pl.ANY),
        scratch_shapes=[
            pltpu.VMEM((6, k_tiles, LANES), F32),
            pltpu.VMEM((half_r, k), BF16),
            pltpu.VMEM((half_r, k), BF16),
            pltpu.VMEM((M, k), F32),
            pltpu.VMEM((M, k), F32),
            pltpu.VMEM((half_c, k), F32),
            pltpu.VMEM((half_c, k), F32),
            pltpu.VMEM((half_c, k), BF16),
            pltpu.VMEM((half_c, k), BF16),
            pltpu.VMEM((5, k_tiles, LANES), F32),
            pltpu.VMEM((2, k_tiles, LANES), jnp.int32),
            pltpu.VMEM((k_tiles, 2, 2, half_r // SUB, LANES), F32),
            pltpu.VMEM((R, C), F32),
            pltpu.VMEM((wide, k), BF16),
            pltpu.VMEM((wide, k), BF16),
            pltpu.VMEM((6 * M, k), BF16),
            pltpu.VMEM((6 * M, k), BF16),
            pltpu.VMEM((2, SUB, k), F32),
            pltpu.VMEM((half_r, wide), F32),
            pltpu.VMEM((half_r, wide), F32),
            pltpu.VMEM((6 * M, half_c), F32),
            pltpu.VMEM((6 * M, half_c), F32),
            pltpu.SemaphoreType.DMA((2 * half_r // M * (half_c // LANES),)),
        ],
        compiler_params=params(36),
        name="image",
    )(blocks, mid, looked)


def solution(mesh):
    return jax.shard_map(
        shards,
        mesh=mesh,
        in_specs=(
            P(None, ("frow", "fcol")),
            P(None, ("frow", "fcol")),
            P(("frow", "fcol")),
            P(),
            P(),
            P("frow", "fcol", None, None),
            P(),
        ),
        out_specs=P("frow", "fcol"),
        check_vma=False,
    )
```

profile of v0, /device:TPU:0, one launch (start us, length us, event | category | flops | bytes accessed | tf_op | source)
XLA Modules:
  0.0 25.0 jit_solution(6655379014111005112)
XLA Ops:
  0.0 1.5 %pack.1 = (f32[32,1,1280]{2,1,0:T(1,128)}, f32[16,128]{1,0:T(8,128)}) custom-call(s32[32]{0:T(128)} %order_ref.1, f32[2,256]{1,0:T(2,128)} %vis_ref.1, s32[2,256]{1,0:T(2,128)} %pair_ref.1, s32[1,256]{1,0:T(1,128)} %bitcast.13, s32[4,128]{1,0:T(4,128)} %bitcast.11, s32[4,128]{1,0:T(4,128)} %bitcast.12), custom_call_target="tpu_custom_call" | custom-call | tf_op jit(solution)/shard_map/pack/pallas_call | solution.py:468
  1.5 3.9 %collective-permute-start.1 = (f32[128,128]{1,0:T(8,128)}, f32[128,128]{1,0:T(8,128)S(1)}, u32[]{:S(2)}, u32[]{:S(2)}) collective-permute-start(f32[128,128]{1,0:T(8,128)} %bitcast.8), channel_id=1, source_target_pairs={{8,16},{16,8},{0,24},{24,0},{9,17},{17,9},{1,25},{25,1},{10,18},{1... | collective-permute-start | bytes 196616 | tf_op jit(solution)/shard_map/ppermute | solution.py:479
  5.4 0.5 %collective-permute-start = (f32[128,128]{1,0:T(8,128)}, f32[128,128]{1,0:T(8,128)S(1)}, u32[]{:S(2)}, u32[]{:S(2)}) collective-permute-start(f32[128,128]{1,0:T(8,128)} %bitcast.9), channel_id=1, source_target_pairs={{0,8},{16,24},{8,0},{24,16},{1,9},{17,25},{9,1},{25,17},{2,10},{18... | collective-permute-start | bytes 196616 | tf_op jit(solution)/shard_map/ppermute | solution.py:479
  5.9 4.9 %all-to-all-start = ((f32[32,1,1280]{2,1,0:T(1,128)}), f32[32,1,1280]{2,1,0:T(1,128)S(1)}, u32[]{:S(2)}, u32[]{:S(2)}) async-start(f32[32,1,1280]{2,1,0:T(1,128)} %get-tuple-element.10), calls=%async_computation | async-start | bytes 327680 | tf_op jit(solution)/shard_map/all_to_all | solution.py:481
  10.8 0.0 collective-permute-done.1
  10.9 0.0 collective-permute-done
  10.9 0.9 %pad_maximum_fusion.mid_ref.cell_ref = f32[400,128]{1,0:T(8,128)S(1)} fusion(f32[16,128]{1,0:T(8,128)} %get-tuple-element.12, f32[128,128]{1,0:T(8,128)S(1)} %collective-permute-done.1, f32[128,128]{1,0:T(8,128)S(1)} %collective-permute-done, f32[128,128]{1,0:T(8,128)} %bitcast.10), kind=kLoop, calls=%fused_computation | loop fusion | flops 153600 | bytes 409600 | tf_op jit(solution)/shard_map/concatenate | solution.py:482
  11.7 1.8 %collective-permute-start.3 = (f32[400,128]{1,0:T(8,128)S(1)}, f32[400,128]{1,0:T(8,128)S(1)}, u32[]{:S(2)}, u32[]{:S(2)}) collective-permute-start(f32[400,128]{1,0:T(8,128)S(1)} %pad_maximum_fusion.mid_ref.cell_ref), channel_id=1, source_target_pairs={{1,2},{3,4},{5,6},{2,1},{4,3},{6,5},{9,10},{11,12},{13,14},{10,9},... | collective-permute-start | bytes 614408 | tf_op jit(solution)/shard_map/ppermute | solution.py:490
  13.6 0.1 collective-permute-start.2
  13.7 4.7 %collective-permute-done.3.b_ref = f32[400,128]{1,0:T(8,128)S(1)} collective-permute-done((f32[400,128]{1,0:T(8,128)S(1)}, f32[400,128]{1,0:T(8,128)S(1)}, u32[]{:S(2)}, u32[]{:S(2)}) %collective-permute-start.3) | collective-permute-done | bytes 204832 | tf_op jit(solution)/shard_map/ppermute | solution.py:490
  18.4 0.0 collective-permute-done.2.a_ref
  18.4 0.4 %gains.1.gain_ref = bf16[640,256]{1,0:T(8,128)(2,1)S(1)} custom-call(f32[400,128]{1,0:T(8,128)S(1)} %pad_maximum_fusion.mid_ref.cell_ref, f32[400,128]{1,0:T(8,128)S(1)} %collective-permute-done.2.a_ref, f32[400,128]{1,0:T(8,128)S(1)} %collective-permute-done.3.b_ref), custom_call_target="tpu_custom_call" | custom-call | tf_op jit(solution)/shard_map/gains/pallas_call | solution.py:494
  18.8 0.6 %all-to-all-done.block_ref = f32[32,1,1280]{2,1,0:T(1,128)S(1)} async-done(((f32[32,1,1280]{2,1,0:T(1,128)}), f32[32,1,1280]{2,1,0:T(1,128)S(1)}, u32[]{:S(2)}, u32[]{:S(2)}) %all-to-all-start) | async-done | bytes 163872 | tf_op jit(solution)/shard_map/all_to_all | solution.py:481
  19.3 5.7 %image.1 = f32[1024,512]{1,0:T(8,128)} custom-call(f32[32,1,1280]{2,1,0:T(1,128)S(1)} %all-to-all-done.block_ref, f32[400,128]{1,0:T(8,128)S(1)} %pad_maximum_fusion.mid_ref.cell_ref, bf16[640,256]{1,0:T(8,128)(2,1)S(1)} %gains.1.gain_ref), custom_call_target="tpu_custom_call" | custom-call | tf_op jit(solution)/shard_map/image/pallas_call | solution.py:502
Async XLA Ops:
  1.5 9.3 %collective-permute-start.1 = (f32[128,128]{1,0:T(8,128)}, f32[128,128]{1,0:T(8,128)S(1)}, u32[]{:S(2)}, u32[]{:S(2)}) collective-permute-start(f32[128,128]{1,0:T(8,128)} %bitcast.8), channel_id=1, source_target_pairs={{8,16},{16,8},{0,24},{24,0},{9,17},{17,9},{1,25},{25,1},{10,18},{1... | collective-permute-start | bytes 196616 | tf_op jit(solution)/shard_map/ppermute | solution.py:479
  5.4 5.5 %collective-permute-start = (f32[128,128]{1,0:T(8,128)}, f32[128,128]{1,0:T(8,128)S(1)}, u32[]{:S(2)}, u32[]{:S(2)}) collective-permute-start(f32[128,128]{1,0:T(8,128)} %bitcast.9), channel_id=1, source_target_pairs={{0,8},{16,24},{8,0},{24,16},{1,9},{17,25},{9,1},{25,17},{2,10},{18... | collective-permute-start | bytes 196616 | tf_op jit(solution)/shard_map/ppermute | solution.py:479
  5.9 13.4 %all-to-all-start = ((f32[32,1,1280]{2,1,0:T(1,128)}), f32[32,1,1280]{2,1,0:T(1,128)S(1)}, u32[]{:S(2)}, u32[]{:S(2)}) async-start(f32[32,1,1280]{2,1,0:T(1,128)} %get-tuple-element.10), calls=%async_computation | async-start | bytes 327680 | tf_op jit(solution)/shard_map/all_to_all | solution.py:481
  11.7 6.6 %collective-permute-start.3 = (f32[400,128]{1,0:T(8,128)S(1)}, f32[400,128]{1,0:T(8,128)S(1)}, u32[]{:S(2)}, u32[]{:S(2)}) collective-permute-start(f32[400,128]{1,0:T(8,128)S(1)} %pad_maximum_fusion.mid_ref.cell_ref), channel_id=1, source_target_pairs={{1,2},{3,4},{5,6},{2,1},{4,3},{6,5},{9,10},{11,12},{13,14},{10,9},... | collective-permute-start | bytes 614408 | tf_op jit(solution)/shard_map/ppermute | solution.py:490
  13.6 4.8 %collective-permute-start.2 = (f32[400,128]{1,0:T(8,128)S(1)}, f32[400,128]{1,0:T(8,128)S(1)}, u32[]{:S(2)}, u32[]{:S(2)}) collective-permute-start(f32[400,128]{1,0:T(8,128)S(1)} %pad_maximum_fusion.mid_ref.cell_ref), channel_id=1, source_target_pairs={{0,1},{2,3},{4,5},{6,7},{1,0},{3,2},{5,4},{7,6},{8,9},{10,11},{12,... | collective-permute-start | bytes 614408 | tf_op jit(solution)/shard_map/ppermute | solution.py:490
where the time goes:
time: 25.4 us; the launch traced here: 25 us
  starting transfers between devices  11.3 us (44%)
  Pallas kernels  7.59 us (30%)
  waiting for transfers between devices  5.26 us (21%)
  other arithmetic  0.87 us (3%)
    pallas_call x1, Pallas kernels, shards(): pl.pallas_call(functools.partial(image_kernel, n_frow, n_fcol, 3 * depth,...  5.71 us
    all_to_all x1, starting transfers between devices, shards(): blocks = lax.all_to_all(packed, ('frow', 'fcol'), 0, 0)  4.89 us
    ppermute x2, waiting for transfers between devices, shards(): lax.ppermute(mid, ('frow', 'fcol'), all_paired([(r * n_fcol + i, r * n_fc...  4.7 us
    ppermute x2, starting transfers between devices, shards(): lax.ppermute(own, 'frow', all_paired(pairs, n_frow, lambda r: n_frow - 1...  4.43 us
    ppermute x2, starting transfers between devices, shards(): lax.ppermute(mid, ('frow', 'fcol'), all_paired([(r * n_fcol + i, r * n_fc...  1.95 us
    pallas_call x1, Pallas kernels, shards(): pl.pallas_call(pack_kernel, out_shape=[shaped(n_frow * n_fcol, 1, 5 * blo...  1.51 us
    concatenate x1, other arithmetic, shards(): mid = jnp.concatenate([own, row_a, row_b, labels], 0)  0.87 us
    all_to_all x1, waiting for transfers between devices, shards(): blocks = lax.all_to_all(packed, ('frow', 'fcol'), 0, 0)  0.55 us
  transfers between devices with their start and end apart: 5, of which 2 were waited for; matrix products, arithmetic and copies ran while one was open for 3% of the time, Pallas kernels for 1%

commit v1 on v0

--- a/solution.py
+++ b/solution.py
@@ -476,12 +476,18 @@
     gains = facet_station_gains[0, 0]
     depth = gains.size // LANES
     own = gains.reshape(2, -1, LANES).transpose(1, 0, 2).reshape(depth, LANES)
-    row_a, row_b = [lax.ppermute(own, "frow", all_paired(pairs, n_frow, lambda r: n_frow - 1 - r))
-                    for pairs in swaps(n_frow)]
+    count = n_frow * n_fcol
+
+    def beside(i):
+        return i ^ 1 if n_fcol % 2 == 0 else i
+
+    row_a, row_b = [
+        lax.ppermute(own, ("frow", "fcol"), all_paired(
+            [(i * n_fcol + c, j * n_fcol + c) for i, j in pairs for c in range(n_fcol)],
+            count, beside))
+        for pairs in swaps(n_frow)]
     blocks = lax.all_to_all(packed, ("frow", "fcol"), 0, 0)
     mid = jnp.concatenate([own, row_a, row_b, labels], 0)
-    count = n_frow * n_fcol
-
     def next_row(i):
         j = i ^ n_fcol if n_fcol & (n_fcol - 1) == 0 else i
         return j if j < count else i

time: 25.4 us -> 25.4 us (level)
  no operation moved by 1% of the time
where the time goes in v1:
time: 25.4 us; the launch traced here: 25 us
  starting transfers between devices  11.2 us (44%)
  Pallas kernels  7.59 us (30%)
  waiting for transfers between devices  5.26 us (21%)
  other arithmetic  0.87 us (3%)
    pallas_call x1, Pallas kernels, shards(): pl.pallas_call(functools.partial(image_kernel, n_frow, n_fcol, 3 * depth,...  5.71 us
    all_to_all x1, starting transfers between devices, shards(): blocks = lax.all_to_all(packed, ('frow', 'fcol'), 0, 0)  4.84 us
    ppermute x2, waiting for transfers between devices, shards(): lax.ppermute(mid, ('frow', 'fcol'), all_paired([(r * n_fcol + i, r * n_fc...  4.7 us
    ppermute x2, starting transfers between devices, shards(): lax.ppermute(own, ('frow', 'fcol'), all_paired([(i * n_fcol + c, j * n_fc...  4.43 us
    ppermute x2, starting transfers between devices, shards(): lax.ppermute(mid, ('frow', 'fcol'), all_paired([(r * n_fcol + i, r * n_fc...  1.95 us
    pallas_call x1, Pallas kernels, shards(): pl.pallas_call(pack_kernel, out_shape=[shaped(n_frow * n_fcol, 1, 5 * blo...  1.51 us
    concatenate x1, other arithmetic, shards(): mid = jnp.concatenate([own, row_a, row_b, labels], 0)  0.87 us
    all_to_all x1, waiting for transfers between devices, shards(): blocks = lax.all_to_all(packed, ('frow', 'fcol'), 0, 0)  0.55 us
  transfers between devices with their start and end apart: 5, of which 2 were waited for; matrix products, arithmetic and copies ran while one was open for 3% of the time, Pallas kernels for 1%

profile of v1, /device:TPU:0, one launch (start us, length us, event | category | flops | bytes accessed | tf_op | source)
XLA Modules:
  0.0 25.0 jit_solution(3628919494149890205)
XLA Ops:
  0.0 1.5 %pack.1 = (f32[32,1,1280]{2,1,0:T(1,128)}, f32[16,128]{1,0:T(8,128)}) custom-call(s32[32]{0:T(128)} %order_ref.1, f32[2,256]{1,0:T(2,128)} %vis_ref.1, s32[2,256]{1,0:T(2,128)} %pair_ref.1, s32[1,256]{1,0:T(1,128)} %bitcast.13, s32[4,128]{1,0:T(4,128)} %bitcast.11, s32[4,128]{1,0:T(4,128)} %bitcast.12), custom_call_target="tpu_custom_call" | custom-call | tf_op jit(solution)/shard_map/pack/pallas_call | solution.py:468
  1.5 0.5 %collective-permute-start.1 = (f32[128,128]{1,0:T(8,128)}, f32[128,128]{1,0:T(8,128)S(1)}, u32[]{:S(2)}, u32[]{:S(2)}) collective-permute-start(f32[128,128]{1,0:T(8,128)} %bitcast.8), channel_id=1, source_target_pairs={{8,16},{9,17},{10,18},{11,19},{12,20},{13,21},{14,22},{15,23},{16,... | collective-permute-start | bytes 196616 | tf_op jit(solution)/shard_map/ppermute | solution.py:485
  2.0 4.0 %collective-permute-start = (f32[128,128]{1,0:T(8,128)}, f32[128,128]{1,0:T(8,128)S(1)}, u32[]{:S(2)}, u32[]{:S(2)}) collective-permute-start(f32[128,128]{1,0:T(8,128)} %bitcast.9), channel_id=1, source_target_pairs={{0,8},{1,9},{2,10},{3,11},{4,12},{5,13},{6,14},{7,15},{16,24},{17,... | collective-permute-start | bytes 196616 | tf_op jit(solution)/shard_map/ppermute | solution.py:485
  5.9 4.8 %all-to-all-start = ((f32[32,1,1280]{2,1,0:T(1,128)}), f32[32,1,1280]{2,1,0:T(1,128)S(1)}, u32[]{:S(2)}, u32[]{:S(2)}) async-start(f32[32,1,1280]{2,1,0:T(1,128)} %get-tuple-element.10), calls=%async_computation | async-start | bytes 327680 | tf_op jit(solution)/shard_map/all_to_all | solution.py:489
  10.8 0.0 collective-permute-done.1
  10.8 0.0 collective-permute-done
  10.8 0.9 %pad_maximum_fusion.mid_ref.cell_ref = f32[400,128]{1,0:T(8,128)S(1)} fusion(f32[16,128]{1,0:T(8,128)} %get-tuple-element.12, f32[128,128]{1,0:T(8,128)S(1)} %collective-permute-done.1, f32[128,128]{1,0:T(8,128)S(1)} %collective-permute-done, f32[128,128]{1,0:T(8,128)} %bitcast.10), kind=kLoop, calls=%fused_computation | loop fusion | flops 153600 | bytes 409600 | tf_op jit(solution)/shard_map/concatenate | solution.py:490
  11.7 1.8 %collective-permute-start.3 = (f32[400,128]{1,0:T(8,128)S(1)}, f32[400,128]{1,0:T(8,128)S(1)}, u32[]{:S(2)}, u32[]{:S(2)}) collective-permute-start(f32[400,128]{1,0:T(8,128)S(1)} %pad_maximum_fusion.mid_ref.cell_ref), channel_id=1, source_target_pairs={{1,2},{3,4},{5,6},{2,1},{4,3},{6,5},{9,10},{11,12},{13,14},{10,9},... | collective-permute-start | bytes 614408 | tf_op jit(solution)/shard_map/ppermute | solution.py:496
  13.5 0.1 collective-permute-start.2
  13.6 4.7 %collective-permute-done.3.b_ref = f32[400,128]{1,0:T(8,128)S(1)} collective-permute-done((f32[400,128]{1,0:T(8,128)S(1)}, f32[400,128]{1,0:T(8,128)S(1)}, u32[]{:S(2)}, u32[]{:S(2)}) %collective-permute-start.3) | collective-permute-done | bytes 204832 | tf_op jit(solution)/shard_map/ppermute | solution.py:496
  18.3 0.0 collective-permute-done.2.a_ref
  18.3 0.4 %gains.1.gain_ref = bf16[640,256]{1,0:T(8,128)(2,1)S(1)} custom-call(f32[400,128]{1,0:T(8,128)S(1)} %pad_maximum_fusion.mid_ref.cell_ref, f32[400,128]{1,0:T(8,128)S(1)} %collective-permute-done.2.a_ref, f32[400,128]{1,0:T(8,128)S(1)} %collective-permute-done.3.b_ref), custom_call_target="tpu_custom_call" | custom-call | tf_op jit(solution)/shard_map/gains/pallas_call | solution.py:500
  18.7 0.6 %all-to-all-done.block_ref = f32[32,1,1280]{2,1,0:T(1,128)S(1)} async-done(((f32[32,1,1280]{2,1,0:T(1,128)}), f32[32,1,1280]{2,1,0:T(1,128)S(1)}, u32[]{:S(2)}, u32[]{:S(2)}) %all-to-all-start) | async-done | bytes 163872 | tf_op jit(solution)/shard_map/all_to_all | solution.py:489
  19.3 5.7 %image.1 = f32[1024,512]{1,0:T(8,128)} custom-call(f32[32,1,1280]{2,1,0:T(1,128)S(1)} %all-to-all-done.block_ref, f32[400,128]{1,0:T(8,128)S(1)} %pad_maximum_fusion.mid_ref.cell_ref, bf16[640,256]{1,0:T(8,128)(2,1)S(1)} %gains.1.gain_ref), custom_call_target="tpu_custom_call" | custom-call | tf_op jit(solution)/shard_map/image/pallas_call | solution.py:508
Async XLA Ops:
  1.5 9.3 %collective-permute-start.1 = (f32[128,128]{1,0:T(8,128)}, f32[128,128]{1,0:T(8,128)S(1)}, u32[]{:S(2)}, u32[]{:S(2)}) collective-permute-start(f32[128,128]{1,0:T(8,128)} %bitcast.8), channel_id=1, source_target_pairs={{8,16},{9,17},{10,18},{11,19},{12,20},{13,21},{14,22},{15,23},{16,... | collective-permute-start | bytes 196616 | tf_op jit(solution)/shard_map/ppermute | solution.py:485
  2.0 8.8 %collective-permute-start = (f32[128,128]{1,0:T(8,128)}, f32[128,128]{1,0:T(8,128)S(1)}, u32[]{:S(2)}, u32[]{:S(2)}) collective-permute-start(f32[128,128]{1,0:T(8,128)} %bitcast.9), channel_id=1, source_target_pairs={{0,8},{1,9},{2,10},{3,11},{4,12},{5,13},{6,14},{7,15},{16,24},{17,... | collective-permute-start | bytes 196616 | tf_op jit(solution)/shard_map/ppermute | solution.py:485
  5.9 13.3 %all-to-all-start = ((f32[32,1,1280]{2,1,0:T(1,128)}), f32[32,1,1280]{2,1,0:T(1,128)S(1)}, u32[]{:S(2)}, u32[]{:S(2)}) async-start(f32[32,1,1280]{2,1,0:T(1,128)} %get-tuple-element.10), calls=%async_computation | async-start | bytes 327680 | tf_op jit(solution)/shard_map/all_to_all | solution.py:489
  11.7 6.6 %collective-permute-start.3 = (f32[400,128]{1,0:T(8,128)S(1)}, f32[400,128]{1,0:T(8,128)S(1)}, u32[]{:S(2)}, u32[]{:S(2)}) collective-permute-start(f32[400,128]{1,0:T(8,128)S(1)} %pad_maximum_fusion.mid_ref.cell_ref), channel_id=1, source_target_pairs={{1,2},{3,4},{5,6},{2,1},{4,3},{6,5},{9,10},{11,12},{13,14},{10,9},... | collective-permute-start | bytes 614408 | tf_op jit(solution)/shard_map/ppermute | solution.py:496
  13.5 4.8 %collective-permute-start.2 = (f32[400,128]{1,0:T(8,128)S(1)}, f32[400,128]{1,0:T(8,128)S(1)}, u32[]{:S(2)}, u32[]{:S(2)}) collective-permute-start(f32[400,128]{1,0:T(8,128)S(1)} %pad_maximum_fusion.mid_ref.cell_ref), channel_id=1, source_target_pairs={{0,1},{2,3},{4,5},{6,7},{1,0},{3,2},{5,4},{7,6},{8,9},{10,11},{12,... | collective-permute-start | bytes 614408 | tf_op jit(solution)/shard_map/ppermute | solution.py:496

commit v2 on v0

--- a/solution.py
+++ b/solution.py
@@ -76,8 +76,7 @@
 
 
 def phase_tables(n_frow, n_fcol, first, n_lines, block_ref, cell_ref,
-                 s_ref, ac_ref, as_ref, ec_ref, es_ref, fc_ref, fs_ref, cc_ref, cs_ref,
-                 q_ref, uv_ref, dr_ref):
+                 s_ref, ac_ref, as_ref, ec_ref, es_ref, q_ref, uv_ref, dr_ref):
     frow_at = lax.axis_index("frow")
     fcol_at = lax.axis_index("fcol")
     half_r, half_c = R // 2, C // 2
@@ -125,36 +124,26 @@
 
     iota = lax.broadcasted_iota(jnp.int32, shape, 0)
 
-    def tables(s):
+    def phases(s, which, modulus, half):
+        freq = jnp.broadcast_to(uv_ref[which, s:s + 1, :], shape)
+        fine = turn(freq * (2 * iota + 1), modulus)
+        middle = turn(freq * (16 * iota), modulus)
+        coarse = turn(freq * (128 * iota), modulus)
+        for a in range(half // 64):
+            top = tuple(jnp.broadcast_to(x[a:a + 1], shape) for x in coarse)
+            both = times(middle, top)
+            for comp in range(2):
+                dr_ref[s, which, comp, 8 * a:8 * a + 8, :] = both[comp]
+        for g in range(half // SUB):
+            step = tuple(jnp.broadcast_to(dr_ref[s, which, comp, g:g + 1, :], shape)
+                         for comp in range(2))
+            yield times(fine, step)
+
+    def rows(s):
         lane = slice(s * LANES, (s + 1) * LANES)
-
-        def phases(which, modulus, half):
-            freq = jnp.broadcast_to(uv_ref[which, s:s + 1, :], shape)
-            fine = turn(freq * (2 * iota + 1), modulus)
-            middle = turn(freq * (16 * iota), modulus)
-            coarse = turn(freq * (128 * iota), modulus)
-            for a in range(half // 64):
-                top = tuple(jnp.broadcast_to(x[a:a + 1], shape) for x in coarse)
-                both = times(middle, top)
-                for comp in range(2):
-                    dr_ref[s, which, comp, 8 * a:8 * a + 8, :] = both[comp]
-            for g in range(half // SUB):
-                step = tuple(jnp.broadcast_to(dr_ref[s, which, comp, g:g + 1, :], shape)
-                             for comp in range(2))
-                yield times(fine, step)
-
-        pairs = {}
-
-        def put(ref, first, group, x):
-            key = (id(ref), first)
-            if group % 2 == 0:
-                pairs[key] = x
-            else:
-                start = first + SUB * (group - 1)
-                ref[start:start + 16, lane] = jnp.concatenate([pairs.pop(key), x], 0).astype(BF16)
-
+        put = putter(lane)
         edge = (half_r - M) // SUB
-        for g, (cos, sin) in enumerate(phases(0, mod_r, half_r)):
+        for g, (cos, sin) in enumerate(phases(s, 0, mod_r, half_r)):
             if g >= edge:
                 mine, other = taper_rows(g, half_r)
                 at = slice((g - edge) * SUB, (g - edge + 1) * SUB)
@@ -163,14 +152,22 @@
                 cos, sin = cos * mine, sin * mine
             put(ac_ref, 0, g, cos)
             put(as_ref, 0, g, sin)
-        for g, (cos, sin) in enumerate(phases(1, mod_c, half_c)):
-            put(cc_ref, 0, g, cos)
-            put(cs_ref, 0, g, sin)
-            at = slice(g * SUB, (g + 1) * SUB)
-            fc_ref[at, lane] = cos
-            fs_ref[at, lane] = sin
-
-    return tables
+
+    return rows, lambda s: phases(s, 1, mod_c, half_c)
+
+
+def putter(lane):
+    pairs = {}
+
+    def put(ref, first, group, x):
+        key = (id(ref), first)
+        if group % 2 == 0:
+            pairs[key] = x
+        else:
+            start = first + SUB * (group - 1)
+            ref[start:start + 16, lane] = jnp.concatenate([pairs.pop(key), x], 0).astype(BF16)
+
+    return put
 
 
 def gain_kernel(depth, mid_ref, a_ref, b_ref, gain_ref):
@@ -197,12 +194,12 @@
 
 
 def image_kernel(n_frow, n_fcol, first, n_lines, depth, block_ref, cell_ref, gain_ref, image_ref,
-                 s_ref, ac_ref, as_ref, ec_ref, es_ref, fc_ref, fs_ref, cc_ref, cs_ref,
+                 s_ref, ac_ref, as_ref, ec_ref, es_ref, cc_ref, cs_ref,
                  q_ref, uv_ref, dr_ref, out_ref, tc_ref, ts_ref, uc_ref, us_ref, w_ref,
                  m1_ref, m2_ref, g1_ref, g2_ref, sems):
-    tables = phase_tables(n_frow, n_fcol, first, n_lines, block_ref, cell_ref, s_ref, ac_ref,
-                          as_ref, ec_ref, es_ref, fc_ref, fs_ref, cc_ref, cs_ref,
-                          q_ref, uv_ref, dr_ref)
+    row_tables, column_phases = phase_tables(
+        n_frow, n_fcol, first, n_lines, block_ref, cell_ref, s_ref, ac_ref, as_ref, ec_ref, es_ref,
+        q_ref, uv_ref, dr_ref)
     frow_at = lax.axis_index("frow")
     r_odd = lax.rem(frow_at, 2) == 1
     fcol_at = lax.axis_index("fcol")
@@ -254,7 +251,7 @@
                                     for i in range(step)], 1)
 
         for i in range(step):
-            tables(p * step + i)
+            row_tables(p * step + i)
         owns, nears = [], []
         for n in range(2):
             hot = jnp.where(line_at == line(2 + n), 1.0, 0.0).astype(BF16)
@@ -277,37 +274,34 @@
         for comp in range(2):
             w_ref[comp, :, lane] = near_w[comp]
 
-        pairs = {}
-
-        def put(ref, first, group, x):
-            key = (id(ref), first)
-            if group % 2 == 0:
-                pairs[key] = x
-            else:
-                start = first + SUB * (group - 1)
-                ref[start:start + 16, lane] = jnp.concatenate([pairs.pop(key), x], 0).astype(BF16)
-
         edge = (half_c - M) // SUB
-        wr, wi = [jnp.broadcast_to(x, shape) for x in own_w]
-        (lr, li), (rr, ri) = weight(LEFT, lane), weight(RIGHT, lane)
-        for g in range(half_c // SUB):
-            at = slice(g * SUB, (g + 1) * SUB)
-            cos, sin = fc_ref[at, lane], fs_ref[at, lane]
-            own = (cos, sin)
-            if g >= edge:
-                mine, other = taper_rows(g, half_c, wide)
-                own = (cos * mine, sin * mine)
-                cos, sin = cos * other, sin * other
-                base = 2 * half_c + M
-                put(tc_ref, base, g - edge, lr * cos + li * sin)
-                put(ts_ref, base, g - edge, lr * sin - li * cos)
-                put(tc_ref, base + 2 * M, g - edge, rr * cos - ri * sin)
-                put(ts_ref, base + 2 * M, g - edge, -(rr * sin + ri * cos))
-            base = g * SUB // LANES * LANES
-            put(tc_ref, base, g, wr * own[0])
-            put(tc_ref, base + LANES, g, -wi * own[1])
-            put(ts_ref, base, g, -wi * own[0])
-            put(ts_ref, base + LANES, g, -wr * own[1])
+        step_w = [weight(LEFT, lane), weight(RIGHT, lane),
+                  [jnp.broadcast_to(x, shape) for x in own_w]]
+        for i in range(step):
+            tile = p * step + i
+            lane = slice(tile * LANES, (tile + 1) * LANES)
+            put = putter(lane)
+            (lr, li), (rr, ri), (wr, wi) = [
+                [x[:, i * LANES:(i + 1) * LANES] for x in w] for w in step_w]
+            for g, (cos, sin) in enumerate(column_phases(tile)):
+                put(cc_ref, 0, g, cos)
+                put(cs_ref, 0, g, sin)
+                own = (cos, sin)
+                if g >= edge:
+                    mine, other = taper_rows(g, half_c)
+                    own = (cos * mine, sin * mine)
+                    cos, sin = cos * other, sin * other
+                    base = 2 * half_c + M
+                    put(tc_ref, base, g - edge, lr * cos + li * sin)
+                    put(ts_ref, base, g - edge, lr * sin - li * cos)
+                    put(tc_ref, base + 2 * M, g - edge, rr * cos - ri * sin)
+                    put(ts_ref, base + 2 * M, g - edge, -(rr * sin + ri * cos))
+                base = g * SUB // LANES * LANES
+                put(tc_ref, base, g, wr * own[0])
+                put(tc_ref, base + LANES, g, -wi * own[1])
+                put(ts_ref, base, g, -wi * own[0])
+                put(ts_ref, base + LANES, g, -wr * own[1])
+        lane = slice(p * wide, (p + 1) * wide)
         for ref in (tc_ref, ts_ref):
             ref[2 * half_c:2 * half_c + M, lane] = zero
             ref[2 * half_c + 2 * M:2 * half_c + 3 * M, lane] = zero
@@ -510,8 +504,6 @@
             pltpu.VMEM((half_r, k), BF16),
             pltpu.VMEM((M, k), F32),
             pltpu.VMEM((M, k), F32),
-            pltpu.VMEM((half_c, k), F32),
-            pltpu.VMEM((half_c, k), F32),
             pltpu.VMEM((half_c, k), BF16),
             pltpu.VMEM((half_c, k), BF16),
             pltpu.VMEM((5, k_tiles, LANES), F32),

time: 25.4 us -> 25.9 us (1.020)
  Pallas kernels: 7.59 us -> 8.01 us
    pallas_call x1, Pallas kernels: 5.71 us -> 6.13 us  [shards(): pl.pallas_call(functools.partial(image_kernel, n_frow, n_fcol, 3 * depth,...]
where the time goes in v2:
time: 25.9 us; the launch traced here: 25.4 us
  starting transfers between devices  11.3 us (44%)
  Pallas kernels  8.01 us (31%)
  waiting for transfers between devices  5.26 us (20%)
  other arithmetic  0.87 us (3%)
    pallas_call x1, Pallas kernels, shards(): pl.pallas_call(functools.partial(image_kernel, n_frow, n_fcol, 3 * depth,...  6.13 us
    all_to_all x1, starting transfers between devices, shards(): blocks = lax.all_to_all(packed, ('frow', 'fcol'), 0, 0)  4.89 us
    ppermute x2, waiting for transfers between devices, shards(): lax.ppermute(mid, ('frow', 'fcol'), all_paired([(r * n_fcol + i, r * n_fc...  4.7 us
    ppermute x2, starting transfers between devices, shards(): lax.ppermute(own, 'frow', all_paired(pairs, n_frow, lambda r: n_frow - 1...  4.43 us
    ppermute x2, starting transfers between devices, shards(): lax.ppermute(mid, ('frow', 'fcol'), all_paired([(r * n_fcol + i, r * n_fc...  1.95 us
    pallas_call x1, Pallas kernels, shards(): pl.pallas_call(pack_kernel, out_shape=[shaped(n_frow * n_fcol, 1, 5 * blo...  1.51 us
    concatenate x1, other arithmetic, shards(): mid = jnp.concatenate([own, row_a, row_b, labels], 0)  0.87 us
    all_to_all x1, waiting for transfers between devices, shards(): blocks = lax.all_to_all(packed, ('frow', 'fcol'), 0, 0)  0.55 us
  transfers between devices with their start and end apart: 5, of which 2 were waited for; matrix products, arithmetic and copies ran while one was open for 3% of the time, Pallas kernels for 1%

profile of v2, /device:TPU:0, one launch (start us, length us, event | category | flops | bytes accessed | tf_op | source)
XLA Modules:
  0.0 25.4 jit_solution(6754609881030523642)
XLA Ops:
  0.0 1.5 %pack.1 = (f32[32,1,1280]{2,1,0:T(1,128)}, f32[16,128]{1,0:T(8,128)}) custom-call(s32[32]{0:T(128)} %order_ref.1, f32[2,256]{1,0:T(2,128)} %vis_ref.1, s32[2,256]{1,0:T(2,128)} %pair_ref.1, s32[1,256]{1,0:T(1,128)} %bitcast.13, s32[4,128]{1,0:T(4,128)} %bitcast.11, s32[4,128]{1,0:T(4,128)} %bitcast.12), custom_call_target="tpu_custom_call" | custom-call | tf_op jit(solution)/shard_map/pack/pallas_call | solution.py:462
  1.5 3.9 %collective-permute-start.1 = (f32[128,128]{1,0:T(8,128)}, f32[128,128]{1,0:T(8,128)S(1)}, u32[]{:S(2)}, u32[]{:S(2)}) collective-permute-start(f32[128,128]{1,0:T(8,128)} %bitcast.8), channel_id=1, source_target_pairs={{8,16},{16,8},{0,24},{24,0},{9,17},{17,9},{1,25},{25,1},{10,18},{1... | collective-permute-start | bytes 196616 | tf_op jit(solution)/shard_map/ppermute | solution.py:473
  5.4 0.5 %collective-permute-start = (f32[128,128]{1,0:T(8,128)}, f32[128,128]{1,0:T(8,128)S(1)}, u32[]{:S(2)}, u32[]{:S(2)}) collective-permute-start(f32[128,128]{1,0:T(8,128)} %bitcast.9), channel_id=1, source_target_pairs={{0,8},{16,24},{8,0},{24,16},{1,9},{17,25},{9,1},{25,17},{2,10},{18... | collective-permute-start | bytes 196616 | tf_op jit(solution)/shard_map/ppermute | solution.py:473
  5.9 4.9 %all-to-all-start = ((f32[32,1,1280]{2,1,0:T(1,128)}), f32[32,1,1280]{2,1,0:T(1,128)S(1)}, u32[]{:S(2)}, u32[]{:S(2)}) async-start(f32[32,1,1280]{2,1,0:T(1,128)} %get-tuple-element.10), calls=%async_computation | async-start | bytes 327680 | tf_op jit(solution)/shard_map/all_to_all | solution.py:475
  10.8 0.0 collective-permute-done.1
  10.9 0.0 collective-permute-done
  10.9 0.9 %pad_maximum_fusion.mid_ref.cell_ref = f32[400,128]{1,0:T(8,128)S(1)} fusion(f32[16,128]{1,0:T(8,128)} %get-tuple-element.12, f32[128,128]{1,0:T(8,128)S(1)} %collective-permute-done.1, f32[128,128]{1,0:T(8,128)S(1)} %collective-permute-done, f32[128,128]{1,0:T(8,128)} %bitcast.10), kind=kLoop, calls=%fused_computation | loop fusion | flops 153600 | bytes 409600 | tf_op jit(solution)/shard_map/concatenate | solution.py:476
  11.7 1.8 %collective-permute-start.3 = (f32[400,128]{1,0:T(8,128)S(1)}, f32[400,128]{1,0:T(8,128)S(1)}, u32[]{:S(2)}, u32[]{:S(2)}) collective-permute-start(f32[400,128]{1,0:T(8,128)S(1)} %pad_maximum_fusion.mid_ref.cell_ref), channel_id=1, source_target_pairs={{1,2},{3,4},{5,6},{2,1},{4,3},{6,5},{9,10},{11,12},{13,14},{10,9},... | collective-permute-start | bytes 614408 | tf_op jit(solution)/shard_map/ppermute | solution.py:484
  13.6 0.1 collective-permute-start.2
  13.7 4.7 %collective-permute-done.3.b_ref = f32[400,128]{1,0:T(8,128)S(1)} collective-permute-done((f32[400,128]{1,0:T(8,128)S(1)}, f32[400,128]{1,0:T(8,128)S(1)}, u32[]{:S(2)}, u32[]{:S(2)}) %collective-permute-start.3) | collective-permute-done | bytes 204832 | tf_op jit(solution)/shard_map/ppermute | solution.py:484
  18.4 0.0 collective-permute-done.2.a_ref
  18.4 0.4 %gains.1.gain_ref = bf16[640,256]{1,0:T(8,128)(2,1)S(1)} custom-call(f32[400,128]{1,0:T(8,128)S(1)} %pad_maximum_fusion.mid_ref.cell_ref, f32[400,128]{1,0:T(8,128)S(1)} %collective-permute-done.2.a_ref, f32[400,128]{1,0:T(8,128)S(1)} %collective-permute-done.3.b_ref), custom_call_target="tpu_custom_call" | custom-call | tf_op jit(solution)/shard_map/gains/pallas_call | solution.py:488
  18.8 0.6 %all-to-all-done.block_ref = f32[32,1,1280]{2,1,0:T(1,128)S(1)} async-done(((f32[32,1,1280]{2,1,0:T(1,128)}), f32[32,1,1280]{2,1,0:T(1,128)S(1)}, u32[]{:S(2)}, u32[]{:S(2)}) %all-to-all-start) | async-done | bytes 163872 | tf_op jit(solution)/shard_map/all_to_all | solution.py:475
  19.3 6.1 %image.1 = f32[1024,512]{1,0:T(8,128)} custom-call(f32[32,1,1280]{2,1,0:T(1,128)S(1)} %all-to-all-done.block_ref, f32[400,128]{1,0:T(8,128)S(1)} %pad_maximum_fusion.mid_ref.cell_ref, bf16[640,256]{1,0:T(8,128)(2,1)S(1)} %gains.1.gain_ref), custom_call_target="tpu_custom_call" | custom-call | tf_op jit(solution)/shard_map/image/pallas_call | solution.py:496
Async XLA Ops:
  1.5 9.3 %collective-permute-start.1 = (f32[128,128]{1,0:T(8,128)}, f32[128,128]{1,0:T(8,128)S(1)}, u32[]{:S(2)}, u32[]{:S(2)}) collective-permute-start(f32[128,128]{1,0:T(8,128)} %bitcast.8), channel_id=1, source_target_pairs={{8,16},{16,8},{0,24},{24,0},{9,17},{17,9},{1,25},{25,1},{10,18},{1... | collective-permute-start | bytes 196616 | tf_op jit(solution)/shard_map/ppermute | solution.py:473
  5.4 5.5 %collective-permute-start = (f32[128,128]{1,0:T(8,128)}, f32[128,128]{1,0:T(8,128)S(1)}, u32[]{:S(2)}, u32[]{:S(2)}) collective-permute-start(f32[128,128]{1,0:T(8,128)} %bitcast.9), channel_id=1, source_target_pairs={{0,8},{16,24},{8,0},{24,16},{1,9},{17,25},{9,1},{25,17},{2,10},{18... | collective-permute-start | bytes 196616 | tf_op jit(solution)/shard_map/ppermute | solution.py:473
  5.9 13.4 %all-to-all-start = ((f32[32,1,1280]{2,1,0:T(1,128)}), f32[32,1,1280]{2,1,0:T(1,128)S(1)}, u32[]{:S(2)}, u32[]{:S(2)}) async-start(f32[32,1,1280]{2,1,0:T(1,128)} %get-tuple-element.10), calls=%async_computation | async-start | bytes 327680 | tf_op jit(solution)/shard_map/all_to_all | solution.py:475
  11.7 6.6 %collective-permute-start.3 = (f32[400,128]{1,0:T(8,128)S(1)}, f32[400,128]{1,0:T(8,128)S(1)}, u32[]{:S(2)}, u32[]{:S(2)}) collective-permute-start(f32[400,128]{1,0:T(8,128)S(1)} %pad_maximum_fusion.mid_ref.cell_ref), channel_id=1, source_target_pairs={{1,2},{3,4},{5,6},{2,1},{4,3},{6,5},{9,10},{11,12},{13,14},{10,9},... | collective-permute-start | bytes 614408 | tf_op jit(solution)/shard_map/ppermute | solution.py:484
  13.6 4.8 %collective-permute-start.2 = (f32[400,128]{1,0:T(8,128)S(1)}, f32[400,128]{1,0:T(8,128)S(1)}, u32[]{:S(2)}, u32[]{:S(2)}) collective-permute-start(f32[400,128]{1,0:T(8,128)S(1)} %pad_maximum_fusion.mid_ref.cell_ref), channel_id=1, source_target_pairs={{0,1},{2,3},{4,5},{6,7},{1,0},{3,2},{5,4},{7,6},{8,9},{10,11},{12,... | collective-permute-start | bytes 614408 | tf_op jit(solution)/shard_map/ppermute | solution.py:484

commit v3 on v0

--- a/solution.py
+++ b/solution.py
@@ -318,10 +318,10 @@
     half_r = R // 2
     n_lane = half_c // LANES
 
-    def own_products(t):
+    def own_products(t, first=0, last=half_r):
         cols = slice(2 * t * LANES, 2 * (t + 1) * LANES if t < n_lane - 1 else tc_ref.shape[0])
-        m1_ref[:, cols] = dot(ac_ref[...], tc_ref[cols, :])
-        m2_ref[:, cols] = dot(as_ref[...], ts_ref[cols, :])
+        m1_ref[first:last, cols] = dot(ac_ref[first:last, :], tc_ref[cols, :])
+        m2_ref[first:last, cols] = dot(as_ref[first:last, :], ts_ref[cols, :])
 
     own_products(n_lane - 1)
     signs = (-1, 1, -1, -1, 1, 1)
@@ -412,15 +412,22 @@
                     out_ref.at[at], image_ref.at[at], sems.at[(j * n_lane + t) * 4 + len(copies)]))
         return copies
 
-    for t in range(n_lane - 2, -1, -1):
-        own_products(t)
-    for t in range(n_lane - 1, -1, -1):
-        for j in range(n_groups):
+    def finish_groups(t, first, last):
+        for j in range(first, last):
             for g in range(j * M // SUB, (j + 1) * M // SUB):
                 finish(g, t, j == n_groups - 1)
             if j % 2:
                 for copy in sends(j // 2, t):
                     copy.start()
+
+    middle = n_groups // 2
+    for t in range(n_lane - 1, -1, -1):
+        if t:
+            own_products(t - 1, 0, half_r // 2)
+        finish_groups(t, 0, middle)
+        if t:
+            own_products(t - 1, half_r // 2, half_r)
+        finish_groups(t, middle, n_groups)
     for t in range(n_lane):
         for j in range(n_groups // 2):
             for copy in sends(j, t):

time: 25.4 us -> 25.3 us (level)
  transfers between devices with their start and end apart: 5 -> 5, of which waited for: 2 -> 2; matrix products, arithmetic and copies ran while one was open for 3% -> 4% of each run, Pallas kernels for 1% -> 1%
where the time goes in v3:
time: 25.3 us; the launch traced here: 24.8 us
  starting transfers between devices  11.3 us (45%)
  Pallas kernels  7.41 us (29%)
  waiting for transfers between devices  5.26 us (21%)
  other arithmetic  0.87 us (3%)
    pallas_call x1, Pallas kernels, shards(): pl.pallas_call(functools.partial(image_kernel, n_frow, n_fcol, 3 * depth,...  5.53 us
    all_to_all x1, starting transfers between devices, shards(): blocks = lax.all_to_all(packed, ('frow', 'fcol'), 0, 0)  4.89 us
    ppermute x2, waiting for transfers between devices, shards(): lax.ppermute(mid, ('frow', 'fcol'), all_paired([(r * n_fcol + i, r * n_fc...  4.7 us
    ppermute x2, starting transfers between devices, shards(): lax.ppermute(own, 'frow', all_paired(pairs, n_frow, lambda r: n_frow - 1...  4.43 us
    ppermute x2, starting transfers between devices, shards(): lax.ppermute(mid, ('frow', 'fcol'), all_paired([(r * n_fcol + i, r * n_fc...  1.95 us
    pallas_call x1, Pallas kernels, shards(): pl.pallas_call(pack_kernel, out_shape=[shaped(n_frow * n_fcol, 1, 5 * blo...  1.51 us
    concatenate x1, other arithmetic, shards(): mid = jnp.concatenate([own, row_a, row_b, labels], 0)  0.87 us
    all_to_all x1, waiting for transfers between devices, shards(): blocks = lax.all_to_all(packed, ('frow', 'fcol'), 0, 0)  0.55 us
  transfers between devices with their start and end apart: 5, of which 2 were waited for; matrix products, arithmetic and copies ran while one was open for 4% of the time, Pallas kernels for 1%

profile of v3, /device:TPU:0, one launch (start us, length us, event | category | flops | bytes accessed | tf_op | source)
XLA Modules:
  0.0 24.8 jit_solution(4683599260410928951)
XLA Ops:
  0.0 1.5 %pack.1 = (f32[32,1,1280]{2,1,0:T(1,128)}, f32[16,128]{1,0:T(8,128)}) custom-call(s32[32]{0:T(128)} %order_ref.1, f32[2,256]{1,0:T(2,128)} %vis_ref.1, s32[2,256]{1,0:T(2,128)} %pair_ref.1, s32[1,256]{1,0:T(1,128)} %bitcast.13, s32[4,128]{1,0:T(4,128)} %bitcast.11, s32[4,128]{1,0:T(4,128)} %bitcast.12), custom_call_target="tpu_custom_call" | custom-call | tf_op jit(solution)/shard_map/pack/pallas_call | solution.py:475
  1.5 3.9 %collective-permute-start.1 = (f32[128,128]{1,0:T(8,128)}, f32[128,128]{1,0:T(8,128)S(1)}, u32[]{:S(2)}, u32[]{:S(2)}) collective-permute-start(f32[128,128]{1,0:T(8,128)} %bitcast.8), channel_id=1, source_target_pairs={{8,16},{16,8},{0,24},{24,0},{9,17},{17,9},{1,25},{25,1},{10,18},{1... | collective-permute-start | bytes 196616 | tf_op jit(solution)/shard_map/ppermute | solution.py:486
  5.4 0.5 %collective-permute-start = (f32[128,128]{1,0:T(8,128)}, f32[128,128]{1,0:T(8,128)S(1)}, u32[]{:S(2)}, u32[]{:S(2)}) collective-permute-start(f32[128,128]{1,0:T(8,128)} %bitcast.9), channel_id=1, source_target_pairs={{0,8},{16,24},{8,0},{24,16},{1,9},{17,25},{9,1},{25,17},{2,10},{18... | collective-permute-start | bytes 196616 | tf_op jit(solution)/shard_map/ppermute | solution.py:486
  5.9 4.9 %all-to-all-start = ((f32[32,1,1280]{2,1,0:T(1,128)}), f32[32,1,1280]{2,1,0:T(1,128)S(1)}, u32[]{:S(2)}, u32[]{:S(2)}) async-start(f32[32,1,1280]{2,1,0:T(1,128)} %get-tuple-element.10), calls=%async_computation | async-start | bytes 327680 | tf_op jit(solution)/shard_map/all_to_all | solution.py:488
  10.8 0.0 collective-permute-done.1
  10.9 0.0 collective-permute-done
  10.9 0.9 %pad_maximum_fusion.mid_ref.cell_ref = f32[400,128]{1,0:T(8,128)S(1)} fusion(f32[16,128]{1,0:T(8,128)} %get-tuple-element.12, f32[128,128]{1,0:T(8,128)S(1)} %collective-permute-done.1, f32[128,128]{1,0:T(8,128)S(1)} %collective-permute-done, f32[128,128]{1,0:T(8,128)} %bitcast.10), kind=kLoop, calls=%fused_computation | loop fusion | flops 153600 | bytes 409600 | tf_op jit(solution)/shard_map/concatenate | solution.py:489
  11.7 1.8 %collective-permute-start.3 = (f32[400,128]{1,0:T(8,128)S(1)}, f32[400,128]{1,0:T(8,128)S(1)}, u32[]{:S(2)}, u32[]{:S(2)}) collective-permute-start(f32[400,128]{1,0:T(8,128)S(1)} %pad_maximum_fusion.mid_ref.cell_ref), channel_id=1, source_target_pairs={{1,2},{3,4},{5,6},{2,1},{4,3},{6,5},{9,10},{11,12},{13,14},{10,9},... | collective-permute-start | bytes 614408 | tf_op jit(solution)/shard_map/ppermute | solution.py:497
  13.6 0.1 collective-permute-start.2
  13.7 4.7 %collective-permute-done.3.b_ref = f32[400,128]{1,0:T(8,128)S(1)} collective-permute-done((f32[400,128]{1,0:T(8,128)S(1)}, f32[400,128]{1,0:T(8,128)S(1)}, u32[]{:S(2)}, u32[]{:S(2)}) %collective-permute-start.3) | collective-permute-done | bytes 204832 | tf_op jit(solution)/shard_map/ppermute | solution.py:497
  18.4 0.0 collective-permute-done.2.a_ref
  18.4 0.4 %gains.1.gain_ref = bf16[640,256]{1,0:T(8,128)(2,1)S(1)} custom-call(f32[400,128]{1,0:T(8,128)S(1)} %pad_maximum_fusion.mid_ref.cell_ref, f32[400,128]{1,0:T(8,128)S(1)} %collective-permute-done.2.a_ref, f32[400,128]{1,0:T(8,128)S(1)} %collective-permute-done.3.b_ref), custom_call_target="tpu_custom_call" | custom-call | tf_op jit(solution)/shard_map/gains/pallas_call | solution.py:501
  18.8 0.6 %all-to-all-done.block_ref = f32[32,1,1280]{2,1,0:T(1,128)S(1)} async-done(((f32[32,1,1280]{2,1,0:T(1,128)}), f32[32,1,1280]{2,1,0:T(1,128)S(1)}, u32[]{:S(2)}, u32[]{:S(2)}) %all-to-all-start) | async-done | bytes 163872 | tf_op jit(solution)/shard_map/all_to_all | solution.py:488
  19.3 5.5 %image.1 = f32[1024,512]{1,0:T(8,128)} custom-call(f32[32,1,1280]{2,1,0:T(1,128)S(1)} %all-to-all-done.block_ref, f32[400,128]{1,0:T(8,128)S(1)} %pad_maximum_fusion.mid_ref.cell_ref, bf16[640,256]{1,0:T(8,128)(2,1)S(1)} %gains.1.gain_ref), custom_call_target="tpu_custom_call" | custom-call | tf_op jit(solution)/shard_map/image/pallas_call | solution.py:509
Async XLA Ops:
  1.5 9.3 %collective-permute-start.1 = (f32[128,128]{1,0:T(8,128)}, f32[128,128]{1,0:T(8,128)S(1)}, u32[]{:S(2)}, u32[]{:S(2)}) collective-permute-start(f32[128,128]{1,0:T(8,128)} %bitcast.8), channel_id=1, source_target_pairs={{8,16},{16,8},{0,24},{24,0},{9,17},{17,9},{1,25},{25,1},{10,18},{1... | collective-permute-start | bytes 196616 | tf_op jit(solution)/shard_map/ppermute | solution.py:486
  5.4 5.5 %collective-permute-start = (f32[128,128]{1,0:T(8,128)}, f32[128,128]{1,0:T(8,128)S(1)}, u32[]{:S(2)}, u32[]{:S(2)}) collective-permute-start(f32[128,128]{1,0:T(8,128)} %bitcast.9), channel_id=1, source_target_pairs={{0,8},{16,24},{8,0},{24,16},{1,9},{17,25},{9,1},{25,17},{2,10},{18... | collective-permute-start | bytes 196616 | tf_op jit(solution)/shard_map/ppermute | solution.py:486
  5.9 13.4 %all-to-all-start = ((f32[32,1,1280]{2,1,0:T(1,128)}), f32[32,1,1280]{2,1,0:T(1,128)S(1)}, u32[]{:S(2)}, u32[]{:S(2)}) async-start(f32[32,1,1280]{2,1,0:T(1,128)} %get-tuple-element.10), calls=%async_computation | async-start | bytes 327680 | tf_op jit(solution)/shard_map/all_to_all | solution.py:488
  11.7 6.6 %collective-permute-start.3 = (f32[400,128]{1,0:T(8,128)S(1)}, f32[400,128]{1,0:T(8,128)S(1)}, u32[]{:S(2)}, u32[]{:S(2)}) collective-permute-start(f32[400,128]{1,0:T(8,128)S(1)} %pad_maximum_fusion.mid_ref.cell_ref), channel_id=1, source_target_pairs={{1,2},{3,4},{5,6},{2,1},{4,3},{6,5},{9,10},{11,12},{13,14},{10,9},... | collective-permute-start | bytes 614408 | tf_op jit(solution)/shard_map/ppermute | solution.py:497
  13.6 4.8 %collective-permute-start.2 = (f32[400,128]{1,0:T(8,128)S(1)}, f32[400,128]{1,0:T(8,128)S(1)}, u32[]{:S(2)}, u32[]{:S(2)}) collective-permute-start(f32[400,128]{1,0:T(8,128)S(1)} %pad_maximum_fusion.mid_ref.cell_ref), channel_id=1, source_target_pairs={{0,1},{2,3},{4,5},{6,7},{1,0},{3,2},{5,4},{7,6},{8,9},{10,11},{12,... | collective-permute-start | bytes 614408 | tf_op jit(solution)/shard_map/ppermute | solution.py:497
